TPU v7x, 32 devices: a whole 2x2x4 slice. The times are simulated.
32 devices in a mesh: groups: 2 (over y), slab: 8 (over z, x), sub: 2 (over core).
Axes of the slice: x: 2, y: 2, z: 4, core: 2. Of those that a mesh axis runs over, the one named last changes fastest.
Arguments:
- fingerprints: bfloat16 [16384, 2048], P(('groups', 'slab', 'sub')), parts along dimension 0, may hold values from 0 to 30, as said below
- coefficients: bfloat16 [16384, 128], P(('groups', 'slab', 'sub')), parts along dimension 0, may hold values from -1.5 to 1.5
- counts: int32 [16], P('groups'), parts along dimension 0, may hold values from 1 to 1024, 6144 in all
- families: int32 [16], P('groups'), parts along dimension 0, may hold values from 0 to 3, never falling along the last dimension, each value on 1 to 3 neighbouring positions
Outputs:
- kernel_product: float32 [16384, 128], P(('groups', 'slab', 'sub')), parts along dimension 0
There are 2 independent parts, one for each index of `groups`. A program takes and returns all parts, laid end to end along the dimension named above; each array names one. Nothing has to cross between parts.
Inputs may be any that keep to these rules, and one draw needn't show every extreme that they name: `counts`: every live pose of a slab comes before its padding slots, and some slab is full. `families`: family ids never fall from one slab to the next, a family spans at most 3 slabs, and some family spans exactly that many. `fingerprints`: entries are non-negative and every fingerprint has a positive entry.
All inputs are finite; a program needn't handle non-finite values.
Results may differ from a plain program's by a relative error of at most 0.0003.
Values may be sent and summed in bfloat16 or wider, within the bound.
A program may use at most 64 MiB of HBM per device.

v0:
```python
import jax
import jax.numpy as jnp
from jax import lax
from jax.sharding import PartitionSpec as P

MOST_SLABS = 3


ridge_weight = 0.5
highest = lax.Precision.HIGHEST


def shifted(value, axis, by):
    count = lax.axis_size(axis)
    pairs = [(i, i + by) for i in range(count) if 0 <= i + by < count]
    return lax.ppermute(value, axis, pairs)


def squared_norms(prints):
    return jnp.sum(jnp.square(prints.astype(jnp.float32)), axis=1)


def tanimoto(row_prints, row_norms, row_valid, col_prints, col_norms, col_valid):
    gram_tile = lax.dot_general(
        row_prints, col_prints, (((1,), (1,)), ((), ())), preferred_element_type=jnp.float32
    )
    kernel = gram_tile / (row_norms[:, None] + col_norms[None, :] - gram_tile)
    return kernel * row_valid[:, None] * col_valid[None, :]


def body(fingerprints, coefficients, counts, families):
    half_rows = fingerprints.shape[0]
    assay_count = coefficients.shape[1]
    slab_count = lax.axis_size("slab")
    slab_place = lax.axis_index("slab")
    half_place = lax.axis_index("sub")
    own_family = families[slab_place]
    full_prints, full_coeffs = (
        lax.all_gather(fingerprints, "sub", axis=0, tiled=True),
        lax.all_gather(coefficients, "sub", axis=0, tiled=True),
    )
    slab_rows = full_prints.shape[0]
    full_norms = squared_norms(full_prints)
    full_valid = (jnp.arange(slab_rows, dtype=jnp.int32) < counts[slab_place]).astype(jnp.float32)
    half_index = half_place * half_rows + jnp.arange(half_rows, dtype=jnp.int32)
    own_norms = lax.dynamic_slice_in_dim(full_norms, half_place * half_rows, half_rows)
    own_valid = (half_index < counts[slab_place]).astype(jnp.float32)
    full_weights = full_coeffs.astype(jnp.float32)
    own_weights = coefficients.astype(jnp.float32)
    diagonal_kernel = tanimoto(
        full_prints, full_norms, full_valid, fingerprints, own_norms, own_valid
    )
    row_total = jnp.dot(diagonal_kernel, own_weights, precision=highest)
    received_total = jnp.zeros((half_rows, assay_count), jnp.float32)
    span_limit = MOST_SLABS - 1
    forward_offsets = list(range(1, span_limit + 1))
    backward_offsets = []
    own_pieces = (fingerprints, coefficients)
    for offset in forward_offsets + [0 - later for later in backward_offsets]:
        pieces = shifted((own_pieces[0], own_pieces[1]), "slab", 0 - offset)
        col_prints, col_coeffs = pieces
        target = slab_place + offset
        inside = jnp.logical_and(target >= 0, target < slab_count)
        clipped = jnp.clip(target, 0, slab_count - 1)
        present = jnp.logical_and(inside, families[clipped] == own_family)
        col_valid = (half_index < counts[clipped]).astype(jnp.float32)

        def compute(operand):
            kernel = tanimoto(
                full_prints,
                full_norms,
                full_valid,
                col_prints,
                squared_norms(col_prints),
                col_valid,
            )
            forward_part = jnp.dot(kernel, col_coeffs.astype(jnp.float32), precision=highest)
            backward_part = lax.dot_general(
                kernel, full_weights, (((0,), (0,)), ((), ())), precision=highest
            )
            return (forward_part, backward_part)

        def skipped(operand):
            return (
                jnp.zeros((slab_rows, assay_count), jnp.float32),
                jnp.zeros((half_rows, assay_count), jnp.float32),
            )

        settle_forward_part, settle_backward_part = lax.cond(present, compute, skipped, 0)
        returned = shifted(settle_backward_part, "slab", offset)
        row_total, received_total = (row_total + settle_forward_part, received_total + returned)
    own_rows = lax.psum_scatter(row_total, "sub", scatter_dimension=0, tiled=True)
    return (own_rows + received_total + ridge_weight * own_weights) * own_valid[:, None]


def solution(mesh):
    in_specs = (
        P(("groups", "slab", "sub"), None),
        P(("groups", "slab", "sub"), None),
        P("groups"),
        P("groups"),
    )
    out_specs = P(("groups", "slab", "sub"), None)
    return jax.shard_map(body, mesh=mesh, in_specs=in_specs, out_specs=out_specs, check_vma=False)
```

profile of v0, /device:TPU:0, one launch (start us, length us, event | category | flops | bytes accessed | tf_op | source)
XLA Modules:
  0.0 154.7 jit_solution(3605313151002196333)
XLA Ops:
  6.5 0.7 all-gather.2.cloned.1.call-update
  7.3 0.0 reduce-scatter.2.cloned.1.call-start
  7.3 1.3 collective-permute-start
  8.6 1.3 collective-permute-start.2
  9.9 1.3 collective-permute-start.1
  11.2 1.3 collective-permute-start.3
  12.5 2.1 %all_gather.7 = bf16[1024,128]{1,0:T(8,128)(2,1)S(1)} all-gather(bf16[512,128]{1,0:T(8,128)(2,1)S(1)} %copy-done.1), channel_id=1, replica_groups=mesh['groups'=2,'slab'=8,'sub'=2] {'sub'}, dimensions={0}, use_global_device_ids=true | all-gather | bytes 393216 | tf_op jit(solution)/shard_map/all_gather | solution.py:40
  14.7 0.7 fusion.19
  18.0 1.1 fusion.17
  19.1 0.7 fusion.18
  19.8 0.7 fusion.16
  20.5 0.7 fusion.12
  21.2 4.1 %all-gather.2.cloned.1.call-done = bf16[1024,2048]{1,0:T(8,128)(2,1)} async-done(((bf16[512,2048]{1,0:T(8,128)(2,1)}), bf16[1024,2048]{1,0:T(8,128)(2,1)}) %all-gather.2.cloned.1.call-update) | async-done | bytes 4194320 | tf_op jit(solution)/shard_map/all_gather | solution.py:39
  25.3 3.2 %multiply_reduce_fusion.2 = f32[1024]{0:T(1024)S(1)} fusion(bf16[1024,2048]{1,0:T(8,128)(2,1)} %all-gather.2.cloned.1.call-done), kind=kLoop, calls=%fused_computation.8 | loop fusion | flops 6290432 | bytes 4198400 | tf_op jit(solution)/shard_map/reduce_sum | solution.py:20
  28.5 0.7 dynamic_slice.22
  29.2 31.6 %collective-permute-done.1 = bf16[512,128]{1,0:T(8,128)(2,1)S(1)} collective-permute-done((bf16[512,128]{1,0:T(8,128)(2,1)S(1)}, bf16[512,128]{1,0:T(8,128)(2,1)S(1)}, u32[]{:S(2)}, u32[]{:S(2)}) %collective-permute-start.1) | collective-permute-done | bytes 131104 | tf_op jit(solution)/shard_map/ppermute | solution.py:16
  60.8 0.0 collective-permute-done
  60.8 0.1 conditional.2
  60.9 48.9 %collective-permute-done.3 = bf16[512,128]{1,0:T(8,128)(2,1)} collective-permute-done((bf16[512,128]{1,0:T(8,128)(2,1)S(1)}, bf16[512,128]{1,0:T(8,128)(2,1)}, u32[]{:S(2)}, u32[]{:S(2)}) %collective-permute-start.3) | collective-permute-done | bytes 131104 | tf_op jit(solution)/shard_map/ppermute | solution.py:16
  109.8 0.0 collective-permute-done.2
  109.8 0.2 conditional.3
  110.1 0.0 copy-start.2
  110.1 5.3 %fusion.25 = f32[1024,512]{1,0:T(8,128)S(1)} fusion(bf16[1024,2048]{1,0:T(8,128)(2,1)} %all-gather.2.cloned.1.call-done, bf16[512,2048]{1,0:T(8,128)(2,1)} %param.8), kind=kOutput, calls=%fused_computation.34 | convolution fusion | flops 2147483648 | bytes 8388608 | tf_op jit(solution)/shard_map/dot_general | solution.py:24
  115.4 1.5 fusion.6
  117.0 0.0 copy-start.3
  117.0 0.9 add_add_fusion
  117.8 0.0 reduce-scatter.2.cloned.1.call-update
  117.9 23.0 %collective-permute-start.4 = (f32[512,128]{1,0:T(8,128)S(1)}, f32[512,128]{1,0:T(8,128)S(1)}, u32[]{:S(2)}, u32[]{:S(2)}) collective-permute-start(f32[512,128]{1,0:T(8,128)S(1)} %get-tuple-element.53), channel_id=1, source_target_pairs={{0,2},{2,4},{4,6},{6,8},{8,10},{10,12},{12,14},{1,3},{3,5},{5,7},{... | collective-permute-start | bytes 786440 | tf_op jit(solution)/shard_map/ppermute | solution.py:16
  140.9 1.3 collective-permute-start.5
  142.2 2.5 %collective-permute-done.4 = f32[512,128]{1,0:T(8,128)S(1)} collective-permute-done((f32[512,128]{1,0:T(8,128)S(1)}, f32[512,128]{1,0:T(8,128)S(1)}, u32[]{:S(2)}, u32[]{:S(2)}) %collective-permute-start.4) | collective-permute-done | bytes 262176 | tf_op jit(solution)/shard_map/ppermute | solution.py:16
  144.7 1.3 collective-permute-done.5
  146.1 1.8 %add_multiply_fusion = f32[512,128]{1,0:T(8,128)} fusion(bf16[512,128]{1,0:T(8,128)(2,1)S(1)} %copy-done.1, f32[512,128]{1,0:T(8,128)} %reduce-scatter.2.cloned.1.call-done, f32[512,128]{1,0:T(8,128)S(1)} %collective-permute-done.4, f32[512,128]{1,0:T(8,128)S(1)} %collective-permute-done.5, f32[512]{0:T(512)S(1)} %fusion.16), kind=kLoop, calls=%fused_computation.18 | loop fusion | flops 393216 | bytes 1181696 | tf_op jit(solution)/shard_map/mul | solution.py:93
  (21 shorter events, 0.2 us)
Async XLA Ops:
  6.5 3.4 %copy-start.1 = (bf16[512,128]{1,0:T(8,128)(2,1)S(1)}, bf16[512,128]{1,0:T(8,128)(2,1)}, u32[]{:S(2)}) copy-start(bf16[512,128]{1,0:T(8,128)(2,1)} %param.9) | copy-start | bytes 393220
  6.5 8.1 %copy-start.4 = (s32[8]{0:T(128)S(1)}, s32[8]{0:T(128)}, u32[]{:S(2)}) copy-start(s32[8]{0:T(128)} %param.10) | copy-start | bytes 100
  6.5 8.1 %copy-start.5 = (s32[8]{0:T(128)S(1)}, s32[8]{0:T(128)}, u32[]{:S(2)}) copy-start(s32[8]{0:T(128)} %param.11) | copy-start | bytes 100
  6.5 18.8 %all-gather.2.cloned.1.call-start = ((), (), s32[]{:S(2)}) async-start(), calls=%async_computation.1 | async-start | bytes 6291456 | tf_op jit(solution)/shard_map/all_gather | solution.py:39
  7.3 138.8 %reduce-scatter.2.cloned.1.call-start = ((), (), s32[]{:S(2)}) async-start(), calls=%async_computation.2 | async-start | bytes 786432 | tf_op jit(solution)/shard_map/reduce_scatter | solution.py:92
  7.3 53.5 %collective-permute-start = (bf16[512,2048]{1,0:T(8,128)(2,1)}, bf16[512,2048]{1,0:T(8,128)(2,1)}, u32[]{:S(2)}, u32[]{:S(2)}) collective-permute-start(bf16[512,2048]{1,0:T(8,128)(2,1)} %param.8), channel_id=1, source_target_pairs={{2,0},{4,2},{6,4},{8,6},{10,8},{12,10},{14,12},{3,1},{5,3},{7,5},{... | collective-permute-start | bytes 6291464 | tf_op jit(solution)/shard_map/ppermute | solution.py:16
  8.6 101.2 %collective-permute-start.2 = (bf16[512,2048]{1,0:T(8,128)(2,1)}, bf16[512,2048]{1,0:T(8,128)(2,1)S(1)}, u32[]{:S(2)}, u32[]{:S(2)}) collective-permute-start(bf16[512,2048]{1,0:T(8,128)(2,1)} %param.8), channel_id=1, source_target_pairs={{4,0},{6,2},{8,4},{10,6},{12,8},{14,10},{5,1},{7,3},{9,5},{11,7},{... | collective-permute-start | bytes 6291464 | tf_op jit(solution)/shard_map/ppermute | solution.py:16
  9.9 50.9 %collective-permute-start.1 = (bf16[512,128]{1,0:T(8,128)(2,1)S(1)}, bf16[512,128]{1,0:T(8,128)(2,1)S(1)}, u32[]{:S(2)}, u32[]{:S(2)}) collective-permute-start(bf16[512,128]{1,0:T(8,128)(2,1)S(1)} %copy-done.1), channel_id=1, source_target_pairs={{2,0},{4,2},{6,4},{8,6},{10,8},{12,10},{14,12},{3,1},{5,3},{7,5},{... | collective-permute-start | bytes 393224 | tf_op jit(solution)/shard_map/ppermute | solution.py:16
  11.2 98.6 %collective-permute-start.3 = (bf16[512,128]{1,0:T(8,128)(2,1)S(1)}, bf16[512,128]{1,0:T(8,128)(2,1)}, u32[]{:S(2)}, u32[]{:S(2)}) collective-permute-start(bf16[512,128]{1,0:T(8,128)(2,1)S(1)} %copy-done.1), channel_id=1, source_target_pairs={{4,0},{6,2},{8,4},{10,6},{12,8},{14,10},{5,1},{7,3},{9,5},{11,7},{... | collective-permute-start | bytes 393224 | tf_op jit(solution)/shard_map/ppermute | solution.py:16
  25.3 35.5 %copy-start = (bf16[1024,2048]{1,0:T(8,128)(2,1)S(1)}, bf16[1024,2048]{1,0:T(8,128)(2,1)}, u32[]{:S(2)}) copy-start(bf16[1024,2048]{1,0:T(8,128)(2,1)} %all-gather.2.cloned.1.call-done) | copy-start | bytes 12582916
  25.3 35.5 %copy-start.6 = (f32[512]{0:T(512)S(1)}, f32[512]{0:T(512)}, u32[]{:S(2)}) copy-start(f32[512]{0:T(512)} %fusion.17) | copy-start | bytes 6148
  110.1 5.3 %copy-start.2 = (f32[512,128]{1,0:T(8,128)}, f32[512,128]{1,0:T(8,128)S(1)}, u32[]{:S(2)}) copy-start(f32[512,128]{1,0:T(8,128)S(1)} %get-tuple-element.54) | copy-start | bytes 786436
  110.1 5.3 %copy-start.7 = (f32[512]{0:T(512)S(1)}, f32[512]{0:T(512)}, u32[]{:S(2)}) copy-start(f32[512]{0:T(512)} %dynamic_slice.22) | copy-start | bytes 6148
  117.0 23.9 %copy-start.3 = (f32[512,128]{1,0:T(8,128)S(1)}, f32[512,128]{1,0:T(8,128)}, u32[]{:S(2)}) copy-start(f32[512,128]{1,0:T(8,128)} %copy-done.2) | copy-start | bytes 786436
  117.9 26.9 %collective-permute-start.4 = (f32[512,128]{1,0:T(8,128)S(1)}, f32[512,128]{1,0:T(8,128)S(1)}, u32[]{:S(2)}, u32[]{:S(2)}) collective-permute-start(f32[512,128]{1,0:T(8,128)S(1)} %get-tuple-element.53), channel_id=1, source_target_pairs={{0,2},{2,4},{4,6},{6,8},{8,10},{10,12},{12,14},{1,3},{3,5},{5,7},{... | collective-permute-start | bytes 786440 | tf_op jit(solution)/shard_map/ppermute | solution.py:16
  140.9 5.2 %collective-permute-start.5 = (f32[512,128]{1,0:T(8,128)S(1)}, f32[512,128]{1,0:T(8,128)S(1)}, u32[]{:S(2)}, u32[]{:S(2)}) collective-permute-start(f32[512,128]{1,0:T(8,128)S(1)} %copy-done.3), channel_id=1, source_target_pairs={{0,4},{2,6},{4,8},{6,10},{8,12},{10,14},{1,5},{3,7},{5,9},{7,11},{... | collective-permute-start | bytes 786440 | tf_op jit(solution)/shard_map/ppermute | solution.py:16
Sparse Core Ops, SparseCore 0:
  8.9 16.3 all-gather.1
  118.0 26.8 reduce-scatter.1
where the time goes:
time: 157 us; the launch traced here: 155 us
  waiting for transfers between devices  89.2 us (57%)
  starting transfers between devices  29.5 us (19%)
  between operations  16.2 us (10%)
  other arithmetic  9.12 us (6%)
  matrix products  6.82 us (4%)
  blocking collectives  2.09 us (1%)
    ppermute x6, waiting for transfers between devices, shifted(): return lax.ppermute(value, axis, pairs)  84.4 us
    ppermute x6, starting transfers between devices, shifted(): return lax.ppermute(value, axis, pairs)  29.5 us
    dot_general x1, matrix products, tanimoto(): lax.dot_general(row_prints, col_prints, (((1,), (1,)), ((), ())), preferr...  5.3 us
    all_gather x1, waiting for transfers between devices, body(): lax.all_gather(fingerprints, 'sub', axis=0, tiled=True)  4.14 us
    reduce_sum x1, other arithmetic, squared_norms(): return jnp.sum(jnp.square(prints.astype(jnp.float32)), axis=1)  3.22 us
  transfers between devices with their start and end apart: 8, of which 5 were waited for; matrix products, arithmetic and copies ran while one was open for 5% of the time, Pallas kernels for 0%

commit v1 on v0

v1 whole, which is shorter than its diff:
```python
import functools

import jax
import jax.numpy as jnp
from jax import lax
from jax.experimental import pallas as pl
from jax.experimental.pallas import tpu as pltpu
from jax.sharding import PartitionSpec as P

STEPS = 4
ridge_weight = 0.5
MESH = pl.DeviceIdType.MESH


def kernel(
    slab_count, feat, prints, coeffs, counts, families, out,
    ob, xb, zb, acc, accz, ret, ocol, zcol, orow, xrow, zrow,
    lsem, osem, xsem, zsem, fxsem, fzsem, rsem,
):
    half = coeffs.shape[0]
    size = half // STEPS
    tile = 2 * size
    s, c = lax.axis_index("slab"), lax.axis_index("sub")
    step_dir = 1 - 2 * lax.rem(s, 2)
    mate = 1 - c
    xs = s + step_dir
    src, dst = s + 2 * step_dir, s - 2 * step_dir
    has_src = jnp.logical_and(src >= 0, src < slab_count)
    has_dst = jnp.logical_and(dst >= 0, dst < slab_count)
    src_at, dst_at = jnp.clip(src, 0, slab_count - 1), jnp.clip(dst, 0, slab_count - 1)

    def own_rows(k):
        return pl.ds(pl.multiple_of(c * half + k * size, 16), size)

    def put_rows(k):
        return pl.ds(pl.multiple_of(k * tile + c * size, 16), size)

    def local(k):
        return pltpu.make_async_copy(
            prints.at[pl.ds(k * size, size), :], ob.at[own_rows(k), pl.ds(0, feat)], lsem.at[k]
        )

    def remote(source, target, sem, k, slab, sub):
        return pltpu.make_async_remote_copy(
            src_ref=source, dst_ref=target, send_sem=sem.at[0, k], recv_sem=sem.at[1, k],
            device_id={"slab": slab, "sub": sub}, device_id_type=MESH,
        )

    def x_copy(k):
        return remote(ob.at[own_rows(k), :], xb.at[put_rows(k), :], xsem, k, xs, c)

    def z_copy(k):
        return remote(ob.at[own_rows(k), :], zb.at[put_rows(k), :], zsem, k, dst_at, c)

    def x_pass(k):
        return remote(xb.at[put_rows(k), :], xb.at[put_rows(k), :], fxsem, k, s, mate)

    def z_pass(k):
        return remote(zb.at[put_rows(k), :], zb.at[put_rows(k), :], fzsem, k, s, mate)

    def o_copy():
        rows = pl.ds(pl.multiple_of(c * half, 16), half)
        return remote(ob.at[rows, :], ob.at[rows, :], osem, 0, s, mate)

    def ret_copy(k):
        rows = pl.ds(k * size, size)
        return remote(accz.at[rows, :], ret.at[rows, :], rsem, k, src_at, c)

    for k in range(STEPS):
        local(k).start()
    barrier = pltpu.get_barrier_semaphore()

    def greet(slab, sub):
        pl.semaphore_signal(
            barrier, inc=1, device_id={"slab": slab, "sub": sub}, device_id_type=MESH
        )

    greet(s, mate)
    greet(xs, c)
    pl.when(has_src)(lambda: greet(src_at, c))
    pl.when(has_dst)(lambda: greet(dst_at, c))

    place = c * half + lax.broadcasted_iota(jnp.int32, coeffs.shape, 0)
    live = place < counts[s]
    weights = jnp.where(live, coeffs[...].astype(jnp.float32), 0.0)
    ob[pl.ds(pl.multiple_of(c * half, 16), half), pl.ds(feat, coeffs.shape[1])] = weights.astype(
        jnp.bfloat16
    )
    pl.semaphore_wait(barrier, 2 + has_src.astype(jnp.int32) + has_dst.astype(jnp.int32))
    for k in range(STEPS):
        local(k).wait()
        x_copy(k).start()
        pl.when(has_dst)(lambda k=k: z_copy(k).start())
    o_copy().start()

    one, zero = jnp.float32(1), jnp.float32(0)
    own_family, x_family, z_family = families[s], families[xs], families[src_at]
    with_x = jnp.where(own_family == x_family, one, zero)
    with_z = jnp.where(own_family == z_family, one, zero)
    x_with_z = jnp.where(x_family == z_family, one, zero)

    def norms(buf, start, count):
        block = buf[pl.ds(start, count), pl.ds(0, feat)].astype(jnp.float32)
        return jnp.sum(block * block, axis=1, keepdims=True)

    def store_row(ref, j, values):
        wide = jnp.broadcast_to(values, (values.shape[0], 128))
        ref[j] = jnp.transpose(wide)[:8, :]

    def piece(rbuf, start, count, col, cbuf, j, row, flag, total, at):
        first = pl.multiple_of(j * tile, 16)
        gram = lax.dot_general(
            rbuf[pl.ds(start, count), pl.ds(0, feat)],
            cbuf[pl.ds(first, tile), pl.ds(0, feat)],
            (((1,), (1,)), ((), ())),
            preferred_element_type=jnp.float32,
        )
        values = gram / (col[pl.ds(at, count), :] + row[j][:1, :] - gram)
        high = values.astype(jnp.bfloat16)
        low = (values - high.astype(jnp.float32)).astype(jnp.bfloat16)
        col_weights = cbuf[pl.ds(first, tile), pl.ds(feat, coeffs.shape[1])]
        part = jnp.dot(high, col_weights, preferred_element_type=jnp.float32)
        part += jnp.dot(low, col_weights, preferred_element_type=jnp.float32)
        total[pl.ds(at, count), :] += part * flag

    def own_by(cbuf, j, row, flag):
        @pl.loop(0, half // tile)
        def _(i):
            at = pl.multiple_of(i * tile, 16)
            piece(ob, pl.multiple_of(c * half + at, 16), tile, ocol, cbuf, j, row, flag, acc, at)

    def z_by(i, cbuf, j, row, flag):
        start = pl.multiple_of(i * tile + c * size, 16)
        piece(zb, start, size, zcol, cbuf, j, row, flag, accz, pl.multiple_of(i * size, 16))

    acc[...] = weights * ridge_weight
    accz[...] = jnp.zeros_like(accz)

    @pl.loop(0, half // tile)
    def _(i):
        at = pl.multiple_of(i * tile, 16)
        ocol[pl.ds(at, tile), :] = norms(ob, pl.multiple_of(c * half + at, 16), tile)

    o_copy().wait_recv()

    @pl.loop(0, 2 * half // tile)
    def _(j):
        store_row(orow, j, norms(ob, pl.multiple_of(j * tile, 16), tile))
        own_by(ob, j, orow, one)

    for k in range(STEPS):
        last = k == STEPS - 1
        x_copy(k).wait_recv()
        x_pass(k).start()

        @pl.when(has_src)
        def _(k=k):
            z_copy(k).wait_recv()
            z_pass(k).start()
            zcol[pl.ds(k * size, size), :] = norms(
                zb, pl.multiple_of(k * tile + c * size, 16), size
            )

            @pl.loop(0, 2 * half // tile)
            def _(j):
                z_by(k, ob, j, orow, with_z)

        x_pass(k).wait_recv()
        store_row(xrow, k, norms(xb, k * tile, tile))

        @pl.when(has_src)
        def _(k=k, last=last):
            for i in range(k):
                z_by(i, xb, k, xrow, x_with_z)
                if last:
                    ret_copy(i).start()

            @pl.loop(0, k + 1)
            def _(j):
                z_by(k, xb, j, xrow, x_with_z)

            if last:
                ret_copy(k).start()
            z_pass(k).wait_recv()
            store_row(zrow, k, norms(zb, k * tile, tile))
            own_by(zb, k, zrow, with_z)

        own_by(xb, k, xrow, with_x)


    @pl.when(has_dst)
    def _():
        for k in range(STEPS):
            ret_copy(k).wait_recv()
        out[...] = jnp.where(live, acc[...] + ret[...], 0.0)

    @pl.when(jnp.logical_not(has_dst))
    def _():
        out[...] = jnp.where(live, acc[...], 0.0)

    o_copy().wait_send()
    for k in range(STEPS):
        x_copy(k).wait_send()
        x_pass(k).wait_send()

        @pl.when(has_dst)
        def _(k=k):
            z_copy(k).wait_send()

        @pl.when(has_src)
        def _(k=k):
            z_pass(k).wait_send()
            ret_copy(k).wait_send()


def body(fingerprints, coefficients, counts, families):
    half, feat = fingerprints.shape
    assays = coefficients.shape[1]
    slab_count = lax.axis_size("slab")
    size = half // STEPS
    tile = 2 * size
    tiles = 2 * half // tile
    bf16, f32 = jnp.bfloat16, jnp.float32
    pair = pltpu.SemaphoreType.DMA((2, STEPS))
    return pl.pallas_call(
        functools.partial(kernel, slab_count, feat),
        out_shape=jax.ShapeDtypeStruct((half, assays), f32),
        in_specs=[
            pl.BlockSpec(memory_space=pl.ANY),
            pl.BlockSpec(memory_space=pltpu.VMEM),
            pl.BlockSpec(memory_space=pltpu.SMEM),
            pl.BlockSpec(memory_space=pltpu.SMEM),
        ],
        out_specs=pl.BlockSpec(memory_space=pltpu.VMEM),
        scratch_shapes=[
            pltpu.VMEM((2 * half, feat + assays), bf16),
            pltpu.VMEM((2 * half, feat + assays), bf16),
            pltpu.VMEM((2 * half, feat + assays), bf16),
            pltpu.VMEM((half, assays), f32),
            pltpu.VMEM((half, assays), f32),
            pltpu.VMEM((half, assays), f32),
            pltpu.VMEM((half, 1), f32),
            pltpu.VMEM((half, 1), f32),
            pltpu.VMEM((tiles, 8, tile), f32),
            pltpu.VMEM((tiles, 8, tile), f32),
            pltpu.VMEM((tiles, 8, tile), f32),
            pltpu.SemaphoreType.DMA((STEPS,)),
            pltpu.SemaphoreType.DMA((2, 1)),
            pair, pair, pair, pair, pair,
        ],
        compiler_params=pltpu.CompilerParams(
            collective_id=0, has_side_effects=True, vmem_limit_bytes=48 * 1024 * 1024
        ),
        cost_estimate=pl.CostEstimate(
            flops=20 * half * half * feat, bytes_accessed=2 * half * feat, transcendentals=0
        ),
    )(fingerprints, coefficients, counts, families)


def solution(mesh):
    in_specs = (
        P(("groups", "slab", "sub"), None),
        P(("groups", "slab", "sub"), None),
        P("groups"),
        P("groups"),
    )
    out_specs = P(("groups", "slab", "sub"), None)
    return jax.shard_map(body, mesh=mesh, in_specs=in_specs, out_specs=out_specs, check_vma=False)
```

time: 157 us -> 70.5 us (0.45); the launches traced: 155 us -> 70.3 us
  waiting for transfers between devices: 89.2 us -> 0 us
  Pallas kernels: 0 us -> 65.8 us
  starting transfers between devices: 29.5 us -> 0 us
  between operations: 16.2 us -> 0.01 us
  other arithmetic: 9.12 us -> 0 us
  matrix products: 6.82 us -> 0 us
  local copies, waits for them, and re-layouts: 1.5 us -> 4.51 us
  blocking collectives: 2.09 us -> 0 us
    ppermute x6 -> x0, waiting for transfers between devices: 84.4 us -> none  [shifted(): return lax.ppermute(value, axis, pairs)]
    pallas_call x0 -> x1, Pallas kernels: none -> 65.8 us  [body(): pl.pallas_call(functools.partial(kernel, slab_count, feat), out_shape=jax...]
    ppermute x6 -> x0, starting transfers between devices: 29.5 us -> none  [shifted(): return lax.ppermute(value, axis, pairs)]
    dot_general x2 -> x0, matrix products: 6.82 us -> none  [the longest x1 5.3 us: tanimoto(): lax.dot_general(row_prints, col_prints, (((1,), (1,)), ((), ())), preferr...]
    unnamed x16 -> x9, local copies, waits for them, and re-layouts: 0.04 us -> 4.51 us
    all_gather x1 -> x0, waiting for transfers between devices: 4.14 us -> none  [body(): lax.all_gather(fingerprints, 'sub', axis=0, tiled=True)]
    convert_element_type x5 -> x0, other arithmetic: 3.23 us -> none  [the longest x2 1.84 us: body(): col_valid = (half_index < counts[clipped]).astype(jnp.float32)]
    reduce_sum x1 -> x0, other arithmetic: 3.22 us -> none  [squared_norms(): return jnp.sum(jnp.square(prints.astype(jnp.float32)), axis=1)]
  transfers between devices with their start and end apart: 8 -> 0, of which waited for: 5 -> 0; matrix products, arithmetic and copies ran while one was open for 5% -> 0% of each run, Pallas kernels for 0% -> 0%
where the time goes in v1:
time: 70.5 us; the launch traced here: 70.3 us
  Pallas kernels  65.8 us (93%)
  local copies, waits for them, and re-layouts  4.51 us (6%)
    pallas_call x1, Pallas kernels, body(): pl.pallas_call(functools.partial(kernel, slab_count, feat), out_shape=jax...  65.8 us
    unnamed x9, local copies, waits for them, and re-layouts  4.51 us

profile of v1, /device:TPU:0, one launch (start us, length us, event | category | flops | bytes accessed | tf_op | source)
XLA Modules:
  0.0 70.3 jit_solution(4037127778499279871)
XLA Ops:
  0.0 0.0 copy-start
  0.0 1.6 %copy-done = bf16[512,2048]{1,0:T(8,128)(2,1)S(1)} copy-done((bf16[512,2048]{1,0:T(8,128)(2,1)S(1)}, bf16[512,2048]{1,0:T(8,128)(2,1)}, u32[]{:S(2)}) %copy-start) | copy-done | bytes 2097176
  1.6 0.0 copy-start.1
  1.6 0.9 %copy-done.1 = bf16[512,128]{1,0:T(8,128)(2,1)S(1)} copy-done((bf16[512,128]{1,0:T(8,128)(2,1)S(1)}, bf16[512,128]{1,0:T(8,128)(2,1)}, u32[]{:S(2)}) %copy-start.1) | copy-done | bytes 131096
  2.5 0.0 copy-start.2
  2.5 0.7 copy-done.2
  3.2 0.0 copy-start.3
  3.2 0.7 copy-done.3
  3.8 65.8 %shard_map.46 = f32[512,128]{1,0:T(8,128)S(1)} custom-call(bf16[512,2048]{1,0:T(8,128)(2,1)S(1)} %copy-done, bf16[512,128]{1,0:T(8,128)(2,1)S(1)} %copy-done.1, s32[8]{0:T(128)S(1)} %copy-done.2, s32[8]{0:T(128)S(1)} %copy-done.3), custom_call_target="tpu_custom_call" | custom-call | flops 10737418240 | bytes 2097152 | tf_op jit(solution)/shard_map/pallas_call | solution.py:225
  69.6 0.7 %copy.6 = f32[512,128]{1,0:T(8,128)} copy(f32[512,128]{1,0:T(8,128)S(1)} %shard_map.46) | data formatting | bytes 524288
Async XLA Ops:
  0.0 1.6 %copy-start = (bf16[512,2048]{1,0:T(8,128)(2,1)S(1)}, bf16[512,2048]{1,0:T(8,128)(2,1)}, u32[]{:S(2)}) copy-start(bf16[512,2048]{1,0:T(8,128)(2,1)} %prints.1) | copy-start | bytes 6291460
  1.6 0.9 %copy-start.1 = (bf16[512,128]{1,0:T(8,128)(2,1)S(1)}, bf16[512,128]{1,0:T(8,128)(2,1)}, u32[]{:S(2)}) copy-start(bf16[512,128]{1,0:T(8,128)(2,1)} %coeffs.1) | copy-start | bytes 393220
  2.5 0.7 copy-start.2
  3.2 0.7 copy-start.3

commit v2 on v1

--- a/solution.py
+++ b/solution.py
@@ -7,15 +7,15 @@
 from jax.experimental.pallas import tpu as pltpu
 from jax.sharding import PartitionSpec as P
 
-STEPS = 4
+STEPS = 2
 ridge_weight = 0.5
 MESH = pl.DeviceIdType.MESH
 
 
 def kernel(
-    slab_count, feat, prints, coeffs, counts, families, out,
+    slab_count, feat, prints, coeffs_in, counts_in, families_in, out,
     ob, xb, zb, acc, accz, ret, ocol, zcol, orow, xrow, zrow,
-    lsem, osem, xsem, zsem, fxsem, fzsem, rsem,
+    coeffs, counts, families, lsem, ssem, osem, xsem, zsem, fxsem, fzsem, rsem,
 ):
     half = coeffs.shape[0]
     size = half // STEPS
@@ -66,6 +66,14 @@
         rows = pl.ds(k * size, size)
         return remote(accz.at[rows, :], ret.at[rows, :], rsem, k, src_at, c)
 
+    small = [
+        pltpu.make_async_copy(source, target, ssem.at[i])
+        for i, (source, target) in enumerate(
+            ((coeffs_in, coeffs), (counts_in, counts), (families_in, families))
+        )
+    ]
+    for copy in small:
+        copy.start()
     for k in range(STEPS):
         local(k).start()
     barrier = pltpu.get_barrier_semaphore()
@@ -80,6 +88,8 @@
     pl.when(has_src)(lambda: greet(src_at, c))
     pl.when(has_dst)(lambda: greet(dst_at, c))
 
+    for copy in small:
+        copy.wait()
     place = c * half + lax.broadcasted_iota(jnp.int32, coeffs.shape, 0)
     live = place < counts[s]
     weights = jnp.where(live, coeffs[...].astype(jnp.float32), 0.0)
@@ -226,10 +236,10 @@
         functools.partial(kernel, slab_count, feat),
         out_shape=jax.ShapeDtypeStruct((half, assays), f32),
         in_specs=[
-            pl.BlockSpec(memory_space=pl.ANY),
-            pl.BlockSpec(memory_space=pltpu.VMEM),
-            pl.BlockSpec(memory_space=pltpu.SMEM),
-            pl.BlockSpec(memory_space=pltpu.SMEM),
+            pl.BlockSpec(memory_space=pltpu.HBM),
+            pl.BlockSpec(memory_space=pltpu.HBM),
+            pl.BlockSpec(memory_space=pltpu.HBM),
+            pl.BlockSpec(memory_space=pltpu.HBM),
         ],
         out_specs=pl.BlockSpec(memory_space=pltpu.VMEM),
         scratch_shapes=[
@@ -244,7 +254,11 @@
             pltpu.VMEM((tiles, 8, tile), f32),
             pltpu.VMEM((tiles, 8, tile), f32),
             pltpu.VMEM((tiles, 8, tile), f32),
+            pltpu.VMEM((half, assays), bf16),
+            pltpu.SMEM(counts.shape, jnp.int32),
+            pltpu.SMEM(families.shape, jnp.int32),
             pltpu.SemaphoreType.DMA((STEPS,)),
+            pltpu.SemaphoreType.DMA((3,)),
             pltpu.SemaphoreType.DMA((2, 1)),
             pair, pair, pair, pair, pair,
         ],

time: 70.5 us -> 68.2 us (0.967)
  Pallas kernels: 65.8 us -> 63.5 us
    pallas_call x1, Pallas kernels: 65.8 us -> 63.5 us  [body(): pl.pallas_call(functools.partial(kernel, slab_count, feat), out_shape=jax...]
where the time goes in v2:
time: 68.2 us; the launch traced here: 68 us
  Pallas kernels  63.5 us (93%)
  local copies, waits for them, and re-layouts  4.51 us (7%)
    pallas_call x1, Pallas kernels, body(): pl.pallas_call(functools.partial(kernel, slab_count, feat), out_shape=jax...  63.5 us
    unnamed x9, local copies, waits for them, and re-layouts  4.51 us

profile of v2, /device:TPU:0, one launch (start us, length us, event | category | flops | bytes accessed | tf_op | source)
XLA Modules:
  0.0 68.0 jit_solution(1780002700262962440)
XLA Ops:
  0.0 0.0 copy-start
  0.0 1.6 %copy-done = bf16[512,2048]{1,0:T(8,128)(2,1)S(1)} copy-done((bf16[512,2048]{1,0:T(8,128)(2,1)S(1)}, bf16[512,2048]{1,0:T(8,128)(2,1)}, u32[]{:S(2)}) %copy-start) | copy-done | bytes 2097176
  1.6 0.0 copy-start.1
  1.6 0.9 %copy-done.1 = bf16[512,128]{1,0:T(8,128)(2,1)S(1)} copy-done((bf16[512,128]{1,0:T(8,128)(2,1)S(1)}, bf16[512,128]{1,0:T(8,128)(2,1)}, u32[]{:S(2)}) %copy-start.1) | copy-done | bytes 131096
  2.5 0.0 copy-start.2
  2.5 0.7 copy-done.2
  3.2 0.0 copy-start.3
  3.2 0.7 copy-done.3
  3.8 63.5 %shard_map.46 = f32[512,128]{1,0:T(8,128)S(1)} custom-call(bf16[512,2048]{1,0:T(8,128)(2,1)S(1)} %copy-done, bf16[512,128]{1,0:T(8,128)(2,1)S(1)} %copy-done.1, s32[8]{0:T(128)S(1)} %copy-done.2, s32[8]{0:T(128)S(1)} %copy-done.3), custom_call_target="tpu_custom_call" | custom-call | flops 10737418240 | bytes 2097152 | tf_op jit(solution)/shard_map/pallas_call | solution.py:235
  67.3 0.7 %copy.6 = f32[512,128]{1,0:T(8,128)} copy(f32[512,128]{1,0:T(8,128)S(1)} %shard_map.46) | data formatting | bytes 524288
Async XLA Ops:
  0.0 1.6 %copy-start = (bf16[512,2048]{1,0:T(8,128)(2,1)S(1)}, bf16[512,2048]{1,0:T(8,128)(2,1)}, u32[]{:S(2)}) copy-start(bf16[512,2048]{1,0:T(8,128)(2,1)} %prints.1) | copy-start | bytes 6291460
  1.6 0.9 %copy-start.1 = (bf16[512,128]{1,0:T(8,128)(2,1)S(1)}, bf16[512,128]{1,0:T(8,128)(2,1)}, u32[]{:S(2)}) copy-start(bf16[512,128]{1,0:T(8,128)(2,1)} %coeffs_in.1) | copy-start | bytes 393220
  2.5 0.7 copy-start.2
  3.2 0.7 copy-start.3

commit v3 on v2

--- a/solution.py
+++ b/solution.py
@@ -175,6 +175,9 @@
             def _(j):
                 z_by(k, ob, j, orow, with_z)
 
+            for j in range(k):
+                z_by(k, xb, j, xrow, x_with_z)
+
         x_pass(k).wait_recv()
         store_row(xrow, k, norms(xb, k * tile, tile))
 
@@ -185,10 +188,7 @@
                 if last:
                     ret_copy(i).start()
 
-            @pl.loop(0, k + 1)
-            def _(j):
-                z_by(k, xb, j, xrow, x_with_z)
-
+            z_by(k, xb, k, xrow, x_with_z)
             if last:
                 ret_copy(k).start()
             z_pass(k).wait_recv()

time: 68.2 us -> 68.3 us (level)
  no operation moved by 1% of the time
where the time goes in v3:
time: 68.3 us; the launch traced here: 68.2 us
  Pallas kernels  63.6 us (93%)
  local copies, waits for them, and re-layouts  4.51 us (7%)
    pallas_call x1, Pallas kernels, body(): pl.pallas_call(functools.partial(kernel, slab_count, feat), out_shape=jax...  63.6 us
    unnamed x9, local copies, waits for them, and re-layouts  4.51 us

profile of v3, /device:TPU:0, one launch (start us, length us, event | category | flops | bytes accessed | tf_op | source)
XLA Modules:
  0.0 68.2 jit_solution(635575917316607627)
XLA Ops:
  0.0 0.0 copy-start
  0.0 1.6 %copy-done = bf16[512,2048]{1,0:T(8,128)(2,1)S(1)} copy-done((bf16[512,2048]{1,0:T(8,128)(2,1)S(1)}, bf16[512,2048]{1,0:T(8,128)(2,1)}, u32[]{:S(2)}) %copy-start) | copy-done | bytes 2097176
  1.6 0.0 copy-start.1
  1.6 0.9 %copy-done.1 = bf16[512,128]{1,0:T(8,128)(2,1)S(1)} copy-done((bf16[512,128]{1,0:T(8,128)(2,1)S(1)}, bf16[512,128]{1,0:T(8,128)(2,1)}, u32[]{:S(2)}) %copy-start.1) | copy-done | bytes 131096
  2.5 0.0 copy-start.2
  2.5 0.7 copy-done.2
  3.2 0.0 copy-start.3
  3.2 0.7 copy-done.3
  3.8 63.6 %shard_map.46 = f32[512,128]{1,0:T(8,128)S(1)} custom-call(bf16[512,2048]{1,0:T(8,128)(2,1)S(1)} %copy-done, bf16[512,128]{1,0:T(8,128)(2,1)S(1)} %copy-done.1, s32[8]{0:T(128)S(1)} %copy-done.2, s32[8]{0:T(128)S(1)} %copy-done.3), custom_call_target="tpu_custom_call" | custom-call | flops 10737418240 | bytes 2097152 | tf_op jit(solution)/shard_map/pallas_call | solution.py:235
  67.5 0.7 %copy.6 = f32[512,128]{1,0:T(8,128)} copy(f32[512,128]{1,0:T(8,128)S(1)} %shard_map.46) | data formatting | bytes 524288
Async XLA Ops:
  0.0 1.6 %copy-start = (bf16[512,2048]{1,0:T(8,128)(2,1)S(1)}, bf16[512,2048]{1,0:T(8,128)(2,1)}, u32[]{:S(2)}) copy-start(bf16[512,2048]{1,0:T(8,128)(2,1)} %prints.1) | copy-start | bytes 6291460
  1.6 0.9 %copy-start.1 = (bf16[512,128]{1,0:T(8,128)(2,1)S(1)}, bf16[512,128]{1,0:T(8,128)(2,1)}, u32[]{:S(2)}) copy-start(bf16[512,128]{1,0:T(8,128)(2,1)} %coeffs_in.1) | copy-start | bytes 393220
  2.5 0.7 copy-start.2
  3.2 0.7 copy-start.3
